TPU v7x, 32 devices: a whole 2x2x4 slice. The times are simulated.
32 devices in a mesh: section: 2 (over core), dp: 16 (over z, y, x).
Axes of the slice: x: 2, y: 2, z: 4, core: 2. Of those that a mesh axis runs over, the one named last changes fastest.
Arguments:
- stream_in: bfloat16 [8192, 767], P('dp'), may hold values from -6 to 6
- cotangent: bfloat16 [8192, 767], P('dp'), may hold values from -6 to 6
- qkv_weight: bfloat16 [2, 768, 2304], P('section'), may hold values from -0.21875 to 0.21875
- out_weight: bfloat16 [2, 768, 767], P('section'), may hold values from -1.75 to 1.75
- up_weight: bfloat16 [2, 768, 3072], P('section'), may hold values from -0.21875 to 0.21875
- down_weight: bfloat16 [2, 3072, 767], P('section'), may hold values from -0.109375 to 0.109375
- attn_gain: float32 [2, 768], P('section'), may hold values from 0.1 to 1.9
- mlp_gain: float32 [2, 768], P('section'), may hold values from 0.1 to 1.9
- seq_lengths: int32 [80], replicated, may hold values from 64 to 256, as said below
- seq_slot: int32 [80], replicated, may hold values from 0 to 31, as said below
Outputs:
- stream_out: bfloat16 [2, 8192, 767], P('section', 'dp')
- stream_grad: bfloat16 [2, 8192, 767], P('section', 'dp')
- qkv_grad: float32 [2, 768, 2304], P('section', 'dp')
- out_grad: float32 [2, 768, 767], P('section', 'dp')
- up_grad: float32 [2, 768, 3072], P('section', 'dp')
- down_grad: float32 [2, 3072, 767], P('section', 'dp')
- attn_gain_grad: float32 [2, 768], P('section', 'dp')
- mlp_gain_grad: float32 [2, 768], P('section', 'dp')
- seq_stats: float32 [2, 80, 2], P('section', 'dp')
Inputs may be any that keep to these rules, and one draw needn't show every extreme that they name: `seq_slot`: slot k is micro-batch k % 2 of data index k // 2; the sequences of a slot, in increasing index order, fill its 256 tokens end to end. Half of the slots hold one sequence of 256 tokens, the others four of 64. `seq_lengths`: each length is 256 or 64, consistent with seq_slot.
All inputs are finite; a program needn't handle non-finite values.
Results may differ from a plain program's by a relative error of at most 0.019.
Values may be sent and summed in bfloat16 or wider, within the bound.
No kernel may reach another device: no remote copies, remote signals or barrier semaphores. Data moves between devices by JAX's collectives and lax.ppermute only.
A program may use at most 192 MiB of HBM per device.

v0:
```python
from functools import partial

import jax
import jax.numpy as jnp
from jax import lax
from jax.sharding import PartitionSpec as P

HD = 64
MICRO = 2


epsilon = 1e-05


def shifted(block, axis, distance):
    devices = range(lax.axis_size(axis))
    route = [(i - distance, i) for i in devices if i - distance in devices]
    return lax.ppermute(block, axis, route)


def rows_product(former, latter):
    return lax.dot_general(
        former, latter, (((0,), (0,)), ((), ())), preferred_element_type=jnp.float32
    )


def against_transposed(former, latter):
    return lax.dot_general(
        former, latter, (((1,), (1,)), ((), ())), preferred_element_type=jnp.float32
    )


def centered_norm(stream):
    row_sum = jnp.sum(stream, axis=1, keepdims=True)
    decompressed = jnp.concatenate([stream, -row_sum], axis=1)
    mean_sq = jnp.mean(decompressed * decompressed, axis=1, keepdims=True)
    factor = lax.rsqrt(mean_sq + epsilon)
    return (decompressed * factor, factor, mean_sq[:, 0])


def centered_norm_back(d_lifted, normed, factor, gain):
    d_normed = d_lifted * gain
    d_gain = jnp.sum(d_lifted * normed, axis=0)
    d_whole = factor * (d_normed - normed * jnp.mean(d_normed * normed, axis=1, keepdims=True))
    return (d_whole[:, :-1] - d_whole[:, -1:], d_gain)


def allowed_keys(begins):
    row_count = begins.shape[0]
    columns = jnp.arange(row_count, dtype=jnp.int32)
    return (columns[None, :] <= columns[:, None]) & (columns[None, :] >= begins[:, None])


def split_heads(packed):
    pieces = packed.reshape(packed.shape[0], 3, -1, HD)
    return (pieces[:, 0], pieces[:, 1], pieces[:, 2])


def masked_scores(queries, key_part, allowed):
    scores = jnp.einsum(
        "qhd,khd->hqk", queries, key_part, preferred_element_type=jnp.float32
    ) * HD ** (-0.5)
    return jnp.where(allowed[None], scores, -1e30)


def attention_forward(packed, begins):
    queries, key_part, values = split_heads(packed)
    scores = masked_scores(queries, key_part, allowed_keys(begins))
    row_peak = jnp.max(scores, axis=2, keepdims=True)
    exponent = jnp.exp(scores - row_peak)
    row_total = jnp.sum(exponent, axis=2, keepdims=True)
    attention = (exponent / row_total).astype(jnp.bfloat16)
    mixed = jnp.einsum("hqk,khd->qhd", attention, values, preferred_element_type=jnp.float32)
    return (mixed.reshape(packed.shape[0], -1).astype(jnp.bfloat16), row_peak + jnp.log(row_total))


def attention_backward(packed, log_total, d_mixed, begins):
    queries, key_part, values = split_heads(packed)
    attention = jnp.exp(masked_scores(queries, key_part, allowed_keys(begins)) - log_total)
    d_heads = d_mixed.reshape(d_mixed.shape[0], -1, HD)
    d_attention = jnp.einsum("qhd,khd->hqk", d_heads, values, preferred_element_type=jnp.float32)
    d_values = jnp.einsum(
        "hqk,qhd->khd", attention.astype(jnp.bfloat16), d_heads, preferred_element_type=jnp.float32
    )
    d_scores = attention * (d_attention - jnp.sum(attention * d_attention, axis=2, keepdims=True))
    d_scores = d_scores.astype(jnp.bfloat16)
    d_queries = jnp.einsum(
        "hqk,khd->qhd", d_scores, key_part, preferred_element_type=jnp.float32
    ) * HD ** (-0.5)
    d_keys = jnp.einsum(
        "hqk,qhd->khd", d_scores, queries, preferred_element_type=jnp.float32
    ) * HD ** (-0.5)
    stacked = jnp.stack([d_queries, d_keys, d_values], axis=1)
    return stacked.reshape(d_mixed.shape[0], -1).astype(jnp.bfloat16)


def layer_forward(stream, begins, weights):
    qkv_w, out_w, up_w, down_w, gain_attn, gain_mlp = weights
    base = stream.astype(jnp.float32)
    normed, factor, attn_square = centered_norm(base)
    lifted = (normed * gain_attn).astype(jnp.bfloat16)
    packed = jnp.dot(lifted, qkv_w, preferred_element_type=jnp.float32).astype(jnp.bfloat16)
    mixed_heads, log_total = attention_forward(packed, begins)
    middle = base + jnp.dot(mixed_heads, out_w, preferred_element_type=jnp.float32)
    normed_mlp, factor_mlp, mlp_square = centered_norm(middle)
    lifted_mlp = (normed_mlp * gain_mlp).astype(jnp.bfloat16)
    hidden = jnp.dot(lifted_mlp, up_w, preferred_element_type=jnp.float32)
    active = jax.nn.gelu(hidden, approximate=True).astype(jnp.bfloat16)
    result = middle + jnp.dot(active, down_w, preferred_element_type=jnp.float32)
    stored = (
        normed,
        factor,
        lifted,
        packed,
        mixed_heads,
        log_total,
        normed_mlp,
        factor_mlp,
        lifted_mlp,
        hidden,
        active,
    )
    return (result, stored, jnp.stack([attn_square, mlp_square], axis=1))


def layer_backward(stored, incoming, begins, weights):
    qkv_w, out_w, up_w, down_w, gain_attn, gain_mlp = weights
    (
        normed,
        factor,
        lifted,
        packed,
        mixed_heads,
        log_total,
        normed_mlp,
        factor_mlp,
        lifted_mlp,
        hidden,
        active,
    ) = stored
    down_part = rows_product(active, incoming)
    d_active = against_transposed(incoming, down_w)
    gelu_value, pullback = jax.vjp(partial(jax.nn.gelu, approximate=True), hidden)
    d_hidden = pullback(d_active)[0].astype(jnp.bfloat16)
    up_part = rows_product(lifted_mlp, d_hidden)
    d_lifted_mlp = against_transposed(d_hidden, up_w)
    d_middle_norm, mlp_gain_part = centered_norm_back(
        d_lifted_mlp, normed_mlp, factor_mlp, gain_mlp
    )
    d_middle = incoming.astype(jnp.float32) + d_middle_norm
    d_branch = d_middle.astype(jnp.bfloat16)
    out_part = rows_product(mixed_heads, d_branch)
    d_heads = against_transposed(d_branch, out_w).astype(jnp.bfloat16)
    d_packed = attention_backward(packed, log_total, d_heads, begins)
    qkv_part = rows_product(lifted, d_packed)
    d_lifted = against_transposed(d_packed, qkv_w)
    d_base_norm, attn_gain_part = centered_norm_back(d_lifted, normed, factor, gain_attn)
    return (
        d_middle + d_base_norm,
        (qkv_part, out_part, up_part, down_part, attn_gain_part, mlp_gain_part),
    )


def shards(
    stream_in,
    cotangent,
    qkv_weight,
    out_weight,
    up_weight,
    down_weight,
    attn_gain,
    mlp_gain,
    seq_lengths,
    seq_slot,
):
    first_section = lax.axis_index("section") == 0
    data_index = lax.axis_index("dp")
    micro_count = MICRO
    row_count = stream_in.shape[0] // micro_count
    compressed = stream_in.shape[1]
    weights = (
        qkv_weight[0],
        out_weight[0],
        up_weight[0],
        down_weight[0],
        attn_gain[0],
        mlp_gain[0],
    )
    inputs = stream_in.reshape(micro_count, row_count, compressed)
    targets = cotangent.reshape(micro_count, row_count, compressed)
    slot_ids = data_index * micro_count + jnp.arange(micro_count, dtype=jnp.int32)
    member = seq_slot[None, :] == slot_ids[:, None]
    held_lengths = jnp.where(member, seq_lengths[None, :], 0)
    starts = jnp.cumsum(held_lengths, axis=1) - held_lengths
    positions = jnp.arange(row_count, dtype=jnp.int32)
    inside = member[:, None, :] & (starts[:, None, :] <= positions[None, :, None])
    begin_table = jnp.max(jnp.where(inside, starts[:, None, :], 0), axis=2)
    owner_table = (member[:, None, :] & (starts[:, None, :] == begin_table[:, :, None])).astype(
        jnp.float32
    )
    received = jnp.zeros((row_count, compressed), jnp.bfloat16)
    section_inputs = []
    results = []
    seq_terms = jnp.zeros((seq_lengths.shape[0], 2), jnp.float32)
    for moment in range(micro_count + 1):
        leading = min(moment, micro_count - 1)
        trailing = max(moment - 1, 0)
        table_index = jnp.where(first_section, leading, trailing)
        begins = begin_table[table_index]
        entering = jnp.where(first_section, inputs[leading], received)
        result, stored, squares = layer_forward(entering, begins, weights)
        leaving = result.astype(jnp.bfloat16)
        usable = jnp.where(first_section, moment < micro_count, moment >= 1)
        tallies = jnp.dot(owner_table[table_index].T, squares, precision=lax.Precision.HIGHEST)
        seq_terms = seq_terms + jnp.where(usable, tallies, 0.0)
        section_inputs.append(entering)
        results.append(leaving)
        if moment < micro_count:
            received = shifted(leaving, "section", 1)
    seq_terms = seq_terms / seq_lengths[:, None].astype(jnp.float32)
    received_grad = jnp.zeros((row_count, compressed), jnp.bfloat16)
    totals = None
    leaving_grads = []
    for moment in range(micro_count + 1):
        source = micro_count - moment
        earliest = max(micro_count - 1 - moment, 0)
        table_index = jnp.where(first_section, min(source, micro_count - 1), earliest)
        begins = begin_table[table_index]
        incoming = jnp.where(first_section, received_grad, targets[earliest])
        stored = layer_forward(section_inputs[source], begins, weights)[1]
        d_input, parts = layer_backward(stored, incoming, begins, weights)
        usable = jnp.where(first_section, moment >= 1, moment < micro_count)
        parts = tuple((jnp.where(usable, member_part, 0.0) for member_part in parts))
        leaving = d_input.astype(jnp.bfloat16)
        leaving_grads.append(leaving)
        totals = parts if totals is None else jax.tree.map(jnp.add, totals, parts)
        if moment < micro_count:
            received_grad = shifted(leaving, "section", -1)
    totals = (
        lax.psum_scatter(totals[0], "dp", scatter_dimension=0, tiled=True),
        lax.psum_scatter(totals[1], "dp", scatter_dimension=0, tiled=True),
        lax.psum_scatter(totals[2], "dp", scatter_dimension=0, tiled=True),
        lax.psum_scatter(totals[3], "dp", scatter_dimension=0, tiled=True),
        lax.psum_scatter(totals[4], "dp", scatter_dimension=0, tiled=True),
        lax.psum_scatter(totals[5], "dp", scatter_dimension=0, tiled=True),
        lax.psum_scatter(seq_terms, "dp", scatter_dimension=0, tiled=True),
    )
    stream_out = jnp.concatenate(
        [
            jnp.where(first_section, results[number], results[number + 1])
            for number in range(micro_count)
        ],
        axis=0,
    )
    stream_grad = jnp.concatenate(
        [
            jnp.where(
                first_section,
                leaving_grads[micro_count - number],
                leaving_grads[micro_count - 1 - number],
            )
            for number in range(micro_count)
        ],
        axis=0,
    )
    return (
        stream_out[None],
        stream_grad[None],
        totals[0][None],
        totals[1][None],
        totals[2][None],
        totals[3][None],
        totals[4][None],
        totals[5][None],
        totals[6][None],
    )


def solution(mesh):
    placed = (
        P("dp", None),
        P("dp", None),
        P("section", None, None),
        P("section", None, None),
        P("section", None, None),
        P("section", None, None),
        P("section", None),
        P("section", None),
        P(),
        P(),
    )
    return jax.shard_map(
        shards,
        mesh=mesh,
        in_specs=placed,
        out_specs=(
            P("section", "dp", None),
            P("section", "dp", None),
            P("section", "dp", None),
            P("section", "dp", None),
            P("section", "dp", None),
            P("section", "dp", None),
            P("section", "dp"),
            P("section", "dp"),
            P("section", "dp", None),
        ),
        check_vma=False,
    )
```

profile of v0, /device:TPU:0, one launch (start us, length us, event | category | flops | bytes accessed | tf_op | source)
XLA Modules:
  0.0 828.1 jit_solution(9050078576522165970)
XLA Ops:
  8.6 1.9 fusion.144
  11.3 1.4 multiply_reduce_fusion.20
  14.0 3.4 convolution_convert_fusion.2
  17.4 2.4 copy.95
  22.8 1.8 fusion.174
  26.8 2.4 fusion.113
  29.9 2.9 fusion.175
  33.6 1.5 multiply_reduce_fusion.19
  36.2 4.1 fusion.22
  40.4 2.0 fusion.108
  42.4 2.9 collective-permute-start
  50.8 3.4 convolution_convert_fusion.1
  54.2 2.4 copy.99
  56.6 1.8 fusion.176
  58.9 2.1 fusion.112
  61.0 1.4 fusion.177
  63.0 1.5 copy.101
  66.4 4.1 fusion.20
  70.6 6.2 broadcast_select_fusion.4
  76.9 2.3 collective-permute-start.1
  82.9 1.5 copy.102
  86.9 3.4 convolution_convert_fusion
  90.3 2.5 copy.103
  92.8 1.8 fusion.178
  95.1 2.1 fusion.111
  99.8 1.5 copy.105
  103.2 4.2 fusion.18
  107.5 6.3 fusion.53
  113.8 2.2 multiply_reduce_fusion.5
  119.9 1.9 copy.106
  121.8 2.7 fusion.78
  124.8 1.8 multiply_reduce_fusion.2
  129.1 2.1 multiply_reduce_fusion.8
  138.4 6.7 fusion.46
  145.2 5.0 multiply_reduce_fusion.4
  154.1 1.9 copy.110
  156.0 2.7 fusion.81
  159.0 1.8 multiply_reduce_fusion.1
  163.6 1.8 multiply_reduce_fusion.7
  167.6 1.5 collective-permute-start.3
  170.2 1.7 collective-permute-done.3
  172.0 3.4 fusion.39
  175.5 2.2 multiply_reduce_fusion.3
  180.1 1.9 select_add_fusion.3
  183.4 5.8 fusion.167
  189.3 4.3 fusion.165
  194.8 1.9 copy.114
  196.8 3.1 multiply_reduce_fusion
  199.9 2.2 multiply_convert_fusion
  205.4 4.7 select_add_fusion.2
  210.4 4.3 fusion.146
  214.8 2.2 fusion.169
  217.0 8.2 select_add_fusion
  225.9 3.4 fusion.168
  229.4 1.5 fusion.166
  230.9 7.1 select_add_fusion.1
  243.7 5.7 fusion.120
  251.1 2.7 multiply_reduce_fusion.6
  253.9 45.0 %all-reduce.3 = (f32[768]{0:T(1024)}, f32[768]{0:T(1024)}, f32[80,2]{0,1:T(2,128)}) all-reduce(f32[768]{0:T(1024)S(1)} %select_add_fusion.5, f32[768]{0:T(1024)S(1)} %select_add_fusion.4, f32[80,2]{0,1:T(2,128)} %fusion.124), channel_id=6, replica_groups=mesh['section'=2,'dp'=16] {'dp'}, use_global_device_ids=true, to_apply=%region_36.37.clone | all-reduce | flops 1696 | bytes 13568
  302.2 1.6 subtract_multiply_fusion
  306.3 5.8 reduce-scatter.8.cloned.1.call-done
  312.1 156.0 %reduce-scatter.6.cloned.1.call-done = f32[48,2304]{1,0:T(8,128)} async-done(((f32[768,2304]{1,0:T(8,128)}), f32[48,2304]{1,0:T(8,128)}) %reduce-scatter.6.cloned.1.call-update) | async-done | bytes 442384 | tf_op jit(solution)/shard_map/reduce_scatter | solution.py:240
  468.1 177.2 %reduce-scatter.12.cloned.1.call-done = f32[192,767]{1,0:T(8,128)} async-done(((f32[3072,767]{1,0:T(8,128)}), f32[192,767]{1,0:T(8,128)}) %reduce-scatter.12.cloned.1.call-update) | async-done | bytes 589072 | tf_op jit(solution)/shard_map/reduce_scatter | solution.py:243
  645.3 176.0 %reduce-scatter.10.cloned.1.call-done = f32[48,3072]{1,0:T(8,128)} async-done(((f32[768,3072]{1,0:T(8,128)}), f32[48,3072]{1,0:T(8,128)}) %reduce-scatter.10.cloned.1.call-update) | async-done | bytes 589840 | tf_op jit(solution)/shard_map/reduce_scatter | solution.py:242
  (394 shorter events, 75.6 us)
Async XLA Ops:
  7.2 6.8 copy-start
  7.2 304.9 %reduce-scatter.8.cloned.1.call-start = ((), (), s32[]{:S(2)}) async-start(), calls=%async_computation.5 | async-start | bytes 2506752 | tf_op jit(solution)/shard_map/reduce_scatter | solution.py:241
  13.3 6.6 copy-start.102
  14.0 5.9 copy-start.121
  20.6 4.5 copy-start.113
  33.6 6.8 slice-start.8
  36.2 4.2 copy-start.27
  36.2 4.2 slice-start.9
  40.4 5.7 copy-start.63
  42.4 5.6 copy-start.125
  42.4 3.7 collective-permute-start
  66.4 4.2 copy-start.17
  66.4 4.2 copy-start.126
  70.6 6.2 copy-start.35
  70.6 8.5 %copy-start.115 = (s32[1,256]{1,0:T(1,128)S(1)}, s32[1,256]{1,0:T(1,128)}, u32[]{:S(2)}) copy-start(s32[1,256]{1,0:T(1,128)} %get-tuple-element.32) | copy-start | bytes 3076
  70.6 9.8 %copy-start.64 = (bf16[512,767]{1,0:T(8,128)(2,1)S(1)}, bf16[512,767]{1,0:T(8,128)(2,1)}, u32[]{:S(2)}) copy-start(bf16[512,767]{1,0:T(8,128)(2,1)} %param.10) | copy-start | bytes 2356228
  76.9 6.0 copy-start.124
  76.9 3.6 collective-permute-start.1
  103.2 12.8 %copy-start.96 = (f32[256]{0:T(256)}, f32[256]{0:T(256)S(1)}, u32[]{:S(2)}) copy-start(f32[256]{0:T(256)S(1)} %get-tuple-element.38) | copy-start | bytes 3076
  103.2 4.2 copy-start.37
  103.2 10.5 %slice-start.4 = ((s8[4718592]{0:T(1024)(128)(4,1)}), s8[4194304]{0:T(1024)(128)(4,1)S(1)}, s32[]{:S(2)}) async-start(s8[4718592]{0:T(1024)(128)(4,1)} %bitcast.333), calls=%async_computation.12 | async-start | bytes 8388608
  107.5 6.3 copy-start.34
  107.5 6.3 copy-start.20
  107.5 6.3 copy-start.73
  107.5 6.3 slice-start.5
  133.3 3.9 collective-permute-start.2
  138.4 12.3 %copy-start.31 = (bf16[256,767]{1,0:T(8,128)(2,1)}, bf16[256,767]{1,0:T(8,128)(2,1)S(1)}, u32[]{:S(2)}) copy-start(bf16[256,767]{1,0:T(8,128)(2,1)S(1)} %broadcast_select_fusion.2) | copy-start | bytes 1178116
  138.4 6.8 copy-start.18
  138.4 6.8 copy-start.69
  145.2 5.1 copy-start.77
  160.8 11.1 %slice-start.10 = ((s8[4718592]{0:T(1024)(128)(4,1)}), s8[4194304]{0:T(1024)(128)(4,1)S(1)}, s32[]{:S(2)}) async-start(s8[4718592]{0:T(1024)(128)(4,1)} %bitcast.339), calls=%async_computation.18 | async-start | bytes 8388608
  163.6 8.4 %slice-start.11 = ((s8[4718592]{0:T(1024)(128)(4,1)}), s8[524288]{0:T(1024)(128)(4,1)S(1)}, s32[]{:S(2)}) async-start(s8[4718592]{0:T(1024)(128)(4,1)} %bitcast.339), calls=%async_computation.19 | async-start | bytes 1048576
  165.4 3.7 copy-start.55
  165.4 3.8 copy-start.82
  167.6 4.3 copy-start.39
  167.6 4.3 copy-start.62
  167.6 4.3 collective-permute-start.3
  169.7 5.8 slice-start.6
  172.0 6.1 copy-start.30
  182.0 286.1 %reduce-scatter.6.cloned.1.call-start = ((), (), s32[]{:S(2)}) async-start(), calls=%async_computation.4 | async-start | bytes 7520256 | tf_op jit(solution)/shard_map/reduce_scatter | solution.py:240
  183.4 5.8 copy-start.15
  183.4 5.8 copy-start.44
  183.4 5.8 copy-start.72
  189.3 4.3 copy-start.11
  189.3 4.3 copy-start.49
  196.8 5.4 copy-start.45
  196.8 8.6 %slice-start.2 = ((s8[7077888]{0:T(1024)(128)(4,1)}), s8[4194304]{0:T(1024)(128)(4,1)S(1)}, s32[]{:S(2)}) async-start(s8[7077888]{0:T(1024)(128)(4,1)} %bitcast.283), calls=%async_computation.10 | async-start | bytes 8388608
  199.9 5.5 slice-start
  199.9 5.5 slice-start.3
  210.2 435.1 %reduce-scatter.12.cloned.1.call-start = ((), (), s32[]{:S(2)}) async-start(), calls=%async_computation.7 | async-start | bytes 10027008 | tf_op jit(solution)/shard_map/reduce_scatter | solution.py:243
  210.4 4.4 copy-start.33
  210.4 4.4 copy-start.36
  225.3 596.1 %reduce-scatter.10.cloned.1.call-start = ((), (), s32[]{:S(2)}) async-start(), calls=%async_computation.6 | async-start | bytes 10027008 | tf_op jit(solution)/shard_map/reduce_scatter | solution.py:242
  238.0 3.8 copy-start.114
  243.5 5.8 copy-start.86
  243.5 6.8 copy-start.122
  243.6 6.7 copy-start.123
  243.6 6.7 copy-start.127
  243.6 7.4 copy-start.13
  243.6 7.4 copy-start.42
  243.6 7.4 copy-start.66
  243.6 7.4 copy-start.104
  298.9 5.2 copy-start.26
  298.9 6.5 copy-start.83
  (84 other events, 172.3 us)
Sparse Core Ops, SparseCore 0:
  182.1 129.9 reduce-scatter.7
  318.9 149.2 reduce-scatter.5
  475.4 169.9 reduce-scatter.11
  651.4 169.8 reduce-scatter.9
where the time goes:
time: 835 us; the launch traced here: 828 us
  waiting for transfers between devices  519 us (62%)
  matrix products  153 us (18%)
  blocking collectives  45 us (5%)
  other arithmetic  43.9 us (5%)
  local copies, waits for them, and re-layouts  42 us (5%)
  between operations  17 us (2%)
  starting transfers between devices  8.58 us (1%)
    reduce_scatter x1, waiting for transfers between devices, shards(): lax.psum_scatter(totals[3], 'dp', scatter_dimension=0, tiled=True)  177 us
    reduce_scatter x1, waiting for transfers between devices, shards(): lax.psum_scatter(totals[2], 'dp', scatter_dimension=0, tiled=True)  176 us
    reduce_scatter x1, waiting for transfers between devices, shards(): lax.psum_scatter(totals[0], 'dp', scatter_dimension=0, tiled=True)  156 us
    unnamed x1, blocking collectives  45 us
    dot_general x12, matrix products, rows_product(): lax.dot_general(former, latter, (((0,), (0,)), ((), ())), preferred_eleme...  44.4 us
    dot_general x12, matrix products, against_transposed(): lax.dot_general(former, latter, (((1,), (1,)), ((), ())), preferred_eleme...  36.2 us
    unnamed x281, local copies, waits for them, and re-layouts  17.8 us
  transfers between devices with their start and end apart: 8, of which 8 were waited for; matrix products, arithmetic and copies ran while one was open for 9% of the time, Pallas kernels for 0%

commit v1 on v0

--- a/solution.py
+++ b/solution.py
@@ -16,6 +16,50 @@
     devices = range(lax.axis_size(axis))
     route = [(i - distance, i) for i in devices if i - distance in devices]
     return lax.ppermute(block, axis, route)
+
+
+def exchanged(block, stride, extent):
+    size = lax.axis_size("dp")
+    place = lambda i: i // stride % extent
+    route = [(i, i + (1 - 2 * place(i)) * stride) for i in range(size)]
+    return lax.ppermute(block.astype(jnp.bfloat16), "dp", route).astype(jnp.float32)
+
+
+def along_pair(blocks, stride, dim):
+    place = lax.axis_index("dp") // stride % 2
+    away = lax.dynamic_index_in_dim(blocks, 1 - place, dim, keepdims=True)
+    own = lax.dynamic_index_in_dim(blocks, place, dim, keepdims=True)
+    return own + exchanged(away, stride, 2)
+
+
+def along_line(blocks, stride, dim):
+    size = lax.axis_size("dp")
+    extent = size // stride
+    place = lax.axis_index("dp") // stride
+    own = lambda s: lax.dynamic_index_in_dim(blocks, jnp.clip(s, 0, extent - 1), dim, keepdims=True)
+    total = own(place)
+    for step in (1, -1):
+        carry = None
+        for turn in range(1, extent):
+            out = own(place + step * (extent - turn))
+            if carry is not None:
+                out = out + carry
+            live = [i for i in range(size) if 0 <= i // stride + step * (extent - turn) < extent]
+            route = [(i, i + step * stride) for i in live]
+            carry = lax.ppermute(out.astype(jnp.bfloat16), "dp", route).astype(jnp.float32)
+        total = total + carry
+    return total
+
+
+def scattered(grads, order):
+    size = lax.axis_size("dp")
+    blocks = grads.reshape(size // 4, 2, 2, grads.shape[0] // size, grads.shape[1])
+    for axis in order:
+        if axis == "z":
+            blocks = along_line(blocks, 4, 0)
+        else:
+            blocks = along_pair(blocks, *((1, 2) if axis == "x" else (2, 1)))
+    return blocks[0, 0, 0]
 
 
 def rows_product(former, latter):
@@ -191,7 +235,9 @@
     slot_ids = data_index * micro_count + jnp.arange(micro_count, dtype=jnp.int32)
     member = seq_slot[None, :] == slot_ids[:, None]
     held_lengths = jnp.where(member, seq_lengths[None, :], 0)
-    starts = jnp.cumsum(held_lengths, axis=1) - held_lengths
+    order = jnp.arange(seq_lengths.shape[0], dtype=jnp.int32)
+    earlier = order[:, None] < order[None, :]
+    starts = jnp.sum(jnp.where(earlier[None], held_lengths[:, :, None], 0), axis=1)
     positions = jnp.arange(row_count, dtype=jnp.int32)
     inside = member[:, None, :] & (starts[:, None, :] <= positions[None, :, None])
     begin_table = jnp.max(jnp.where(inside, starts[:, None, :], 0), axis=2)
@@ -199,7 +245,7 @@
         jnp.float32
     )
     received = jnp.zeros((row_count, compressed), jnp.bfloat16)
-    section_inputs = []
+    kept = []
     results = []
     seq_terms = jnp.zeros((seq_lengths.shape[0], 2), jnp.float32)
     for moment in range(micro_count + 1):
@@ -213,7 +259,7 @@
         usable = jnp.where(first_section, moment < micro_count, moment >= 1)
         tallies = jnp.dot(owner_table[table_index].T, squares, precision=lax.Precision.HIGHEST)
         seq_terms = seq_terms + jnp.where(usable, tallies, 0.0)
-        section_inputs.append(entering)
+        kept.append(stored)
         results.append(leaving)
         if moment < micro_count:
             received = shifted(leaving, "section", 1)
@@ -227,8 +273,7 @@
         table_index = jnp.where(first_section, min(source, micro_count - 1), earliest)
         begins = begin_table[table_index]
         incoming = jnp.where(first_section, received_grad, targets[earliest])
-        stored = layer_forward(section_inputs[source], begins, weights)[1]
-        d_input, parts = layer_backward(stored, incoming, begins, weights)
+        d_input, parts = layer_backward(kept[source], incoming, begins, weights)
         usable = jnp.where(first_section, moment >= 1, moment < micro_count)
         parts = tuple((jnp.where(usable, member_part, 0.0) for member_part in parts))
         leaving = d_input.astype(jnp.bfloat16)
@@ -237,10 +282,10 @@
         if moment < micro_count:
             received_grad = shifted(leaving, "section", -1)
     totals = (
-        lax.psum_scatter(totals[0], "dp", scatter_dimension=0, tiled=True),
-        lax.psum_scatter(totals[1], "dp", scatter_dimension=0, tiled=True),
-        lax.psum_scatter(totals[2], "dp", scatter_dimension=0, tiled=True),
-        lax.psum_scatter(totals[3], "dp", scatter_dimension=0, tiled=True),
+        scattered(totals[0], "xyz"),
+        scattered(totals[1], "yxz"),
+        scattered(totals[2], "yzx"),
+        scattered(totals[3], "xzy"),
         lax.psum_scatter(totals[4], "dp", scatter_dimension=0, tiled=True),
         lax.psum_scatter(totals[5], "dp", scatter_dimension=0, tiled=True),
         lax.psum_scatter(seq_terms, "dp", scatter_dimension=0, tiled=True),

time: 835 us -> 509 us (0.61)
  waiting for transfers between devices: 519 us -> 115 us
  starting transfers between devices: 8.58 us -> 69.8 us
  other arithmetic: 43.9 us -> 59.8 us
  between operations: 17 us -> 4.49 us
  local copies, waits for them, and re-layouts: 42 us -> 53.7 us
    reduce_scatter x4 -> x0, waiting for transfers between devices: 515 us -> none  [the longest x1 177 us: shards(): lax.psum_scatter(totals[3], 'dp', scatter_dimension=0, tiled=True)]
    ppermute x0 -> x32, waiting for transfers between devices: none -> 115 us  [the longest x8 60.8 us: exchanged(): lax.ppermute(block.astype(jnp.bfloat16), 'dp', route).astype(jnp.float32)]
    ppermute x0 -> x32, starting transfers between devices: none -> 61.3 us  [the longest x24 52 us: along_line(): lax.ppermute(out.astype(jnp.bfloat16), 'dp', route).astype(jnp.float32)]
    add x0 -> x8, other arithmetic: none -> 11.9 us  [the longest x6 11.5 us: along_pair(): return own + exchanged(away, stride, 2)]
    convert_element_type x0 -> x12, local copies, waits for them, and re-layouts: none -> 11.7 us  [the longest x8 10.7 us: exchanged(): block.astype(jnp.bfloat16)]
    dot_general x12, matrix products: 44.4 us -> 55.9 us  [rows_product(): lax.dot_general(former, latter, (((0,), (0,)), ((), ())), preferred_eleme...]
    dot_general x12, matrix products: 36.2 us -> 25.4 us  [against_transposed(): lax.dot_general(former, latter, (((1,), (1,)), ((), ())), preferred_eleme...]
    unnamed x281 -> x323, local copies, waits for them, and re-layouts: 17.8 us -> 19.4 us
  transfers between devices with their start and end apart: 8 -> 36, of which waited for: 8 -> 14; matrix products, arithmetic and copies ran while one was open for 9% -> 15% of each run, Pallas kernels for 0% -> 0%
where the time goes in v1:
time: 509 us; the launch traced here: 500 us
  matrix products  156 us (31%)
  waiting for transfers between devices  115 us (23%)
  starting transfers between devices  69.8 us (14%)
  other arithmetic  59.8 us (12%)
  local copies, waits for them, and re-layouts  53.7 us (11%)
  blocking collectives  41 us (8%)
    ppermute x8, waiting for transfers between devices, exchanged(): lax.ppermute(block.astype(jnp.bfloat16), 'dp', route).astype(jnp.float32)  60.8 us
    dot_general x12, matrix products, rows_product(): lax.dot_general(former, latter, (((0,), (0,)), ((), ())), preferred_eleme...  55.9 us
    ppermute x24, waiting for transfers between devices, along_line(): lax.ppermute(out.astype(jnp.bfloat16), 'dp', route).astype(jnp.float32)  54.2 us
    ppermute x24, starting transfers between devices, along_line(): lax.ppermute(out.astype(jnp.bfloat16), 'dp', route).astype(jnp.float32)  52 us
    unnamed x1, blocking collectives  41 us
    dot_general x12, matrix products, against_transposed(): lax.dot_general(former, latter, (((1,), (1,)), ((), ())), preferred_eleme...  25.4 us
    unnamed x323, local copies, waits for them, and re-layouts  19.4 us
    dot_general x3, matrix products, layer_forward(): jnp.dot(active, down_w, preferred_element_type=jnp.float32)  15.2 us
  transfers between devices with their start and end apart: 36, of which 14 were waited for; matrix products, arithmetic and copies ran while one was open for 15% of the time, Pallas kernels for 0%

profile of v1, /device:TPU:0, one launch (start us, length us, event | category | flops | bytes accessed | tf_op | source)
XLA Modules:
  0.0 500.2 jit_solution(17199053746751175860)
XLA Ops:
  7.4 3.4 convolution_convert_fusion.2
  10.8 2.4 copy.95
  19.5 2.4 fusion.113
  21.9 2.9 fusion.174
  28.3 4.1 fusion.22
  32.6 2.7 fusion.108
  35.3 3.2 collective-permute-start
  54.1 3.4 convolution_convert_fusion.1
  57.5 2.4 copy.99
  62.1 2.1 fusion.112
  67.9 4.1 fusion.20
  72.1 6.3 %broadcast_select_fusion.4 = (bf16[256,767]{1,0:T(8,128)(2,1)}, bf16[256,767]{1,0:T(8,128)(2,1)S(1)}) fusion(bf16[256,767]{1,0:T(8,128)(2,1)} %fusion.108, pred[]{:T(512)S(6)} %eq.44, f32[256,767]{1,0:T(8,128)S(1)} %copy-done.17, bf16[1,3072,767]{2,1,0:T(8,128)(2,1)} %param.15, f32[256,3072]{1,0:T(8,128)S(1)} %fusion.20), kind=kOutput, calls=%fused_computation.260 | convolution fusion | flops 1214053632 | bytes 9821697 | tf_op jit(solution)/shard_map/dot_general | solution.py:153
  87.8 3.4 convolution_convert_fusion
  91.1 2.4 copy.103
  95.8 2.1 fusion.111
  104.0 4.2 fusion.18
  108.3 6.2 %fusion.120 = bf16[256,767]{1,0:T(8,128)(2,1)} fusion(bf16[256,767]{1,0:T(8,128)(2,1)S(1)} %copy-done.130, f32[256,767]{1,0:T(8,128)S(1)} %copy-done.20, bf16[1,3072,767]{2,1,0:T(8,128)(2,1)} %param.15, pred[]{:T(512)S(6)} %eq.44, f32[256,3072]{1,0:T(8,128)S(1)} %fusion.18), kind=kOutput, calls=%fused_computation.166 | convolution fusion | flops 1214053632 | bytes 9428993 | tf_op jit(solution)/shard_map/dot_general | solution.py:153
  114.6 3.4 fusion.53
  118.1 2.2 multiply_reduce_fusion.5
  126.0 2.7 fusion.78
  135.1 5.0 %fusion.167 = f32[768,3072]{1,0:T(8,128)} fusion(bf16[256,3072]{1,0:T(8,128)(2,1)S(1)} %copy-done.78, f32[256]{0:T(256)S(1)} %copy-done.109, f32[768]{0:T(1024)S(1)} %reduce.1, f32[256,1]{1,0:T(8,128)S(1)} %copy-done.75, f32[256,767]{1,0:T(8,128)S(1)} %copy-done.21), kind=kOutput, calls=%fused_computation.345 | convolution fusion | flops 1208745984 | bytes 11800576 | tf_op jit(solution)/shard_map/dot_general | solution.py:66
  140.2 6.0 %fusion.146 = f32[3072,767]{1,0:T(8,128)} fusion(bf16[512,767]{1,0:T(8,128)(2,1)S(1)} %copy-done.45, pred[]{:T(512)S(6)} %eq.44, f32[256,3072]{1,0:T(8,128)S(1)} %copy-done.40), kind=kOutput, calls=%fused_computation.290 | convolution fusion | flops 1213660928 | bytes 12963841 | tf_op jit(solution)/shard_map/dot_general | solution.py:66
  153.1 4.8 fusion.166
  158.1 3.0 fusion.46
  161.1 2.1 multiply_reduce_fusion.4
  169.0 2.7 fusion.81
  178.1 5.1 %fusion.165 = f32[768,3072]{1,0:T(8,128)} fusion(bf16[256,3072]{1,0:T(8,128)(2,1)S(1)} %copy-done.80, f32[256]{0:T(256)S(1)} %get-tuple-element.58, f32[768]{0:T(1024)S(1)} %reduce.1, f32[256,1]{1,0:T(8,128)S(1)} %copy-done.72, f32[256,767]{1,0:T(8,128)S(1)} %copy-done.19), kind=kOutput, calls=%fused_computation.343 | convolution fusion | flops 1208745984 | bytes 11800576 | tf_op jit(solution)/shard_map/dot_general | solution.py:66
  183.2 5.8 %fusion.168 = f32[3072,767]{1,0:T(8,128)} fusion(bf16[256,767]{1,0:T(8,128)(2,1)S(1)} %copy-done.38, f32[256,3072]{1,0:T(8,128)S(1)} %copy-done.43), kind=kOutput, calls=%fused_computation.346 | convolution fusion | flops 1213464576 | bytes 12963328 | tf_op jit(solution)/shard_map/dot_general | solution.py:66
  195.3 4.3 fusion.164
  199.8 3.0 fusion.39
  202.8 2.1 multiply_reduce_fusion.3
  210.1 2.7 fusion.84
  217.6 2.1 multiply_reduce_fusion.6
  224.2 2.3 collective-permute-start.4
  229.6 2.4 collective-permute-start.12
  232.1 10.2 %select_add_fusion.1 = f32[768,3072]{1,0:T(8,128)} fusion(f32[768,3072]{1,0:T(8,128)} %fusion.165, f32[768,3072]{1,0:T(8,128)} %fusion.167, bf16[256,3072]{1,0:T(8,128)(2,1)} %copy-done.76, pred[]{:T(512)S(6)} %eq.44, pred[]{:T(512)S(6)} %select_n.329, f32[768]{0:T(1024)S(1)} %reduce.1, f32[256]{0:T(256)S(1)} %copy-done.114, f32[256,1]{1,0:T(8,128)S(1)} %copy-done.69, ...), kind=kOutput, calls=%fused_computation.1 | convolution fusion | flops 1218183168 | bytes 30674946 | tf_op jit(solution)/shard_map/dot_general | solution.py:66
  242.3 4.1 dynamic-slice_convert_fusion.1
  247.4 8.5 %select_add_fusion = f32[3072,767]{1,0:T(8,128)} fusion(f32[3072,767]{1,0:T(8,128)S(1)} %bitcast.292, f32[3072,767]{1,0:T(8,128)S(1)} %bitcast.290, bf16[256,767]{1,0:T(8,128)(2,1)} %copy-done.35, pred[]{:T(512)S(6)} %eq.44, pred[]{:T(512)S(6)} %select_n.329, f32[256,3072]{1,0:T(8,128)} %copy-done.64), kind=kOutput, calls=%fused_computation | convolution fusion | flops 1222889472 | bytes 31813122 | tf_op jit(solution)/shard_map/dot_general | solution.py:66
  255.9 4.2 dynamic-slice_convert_fusion
  264.9 57.8 %collective-permute-done.13 = bf16[4,1,1,48,767]{4,3,2,1,0:T(8,128)(2,1)S(1)} collective-permute-done((bf16[4,1,1,48,767]{4,3,2,1,0:T(8,128)(2,1)S(1)}, bf16[4,1,1,48,767]{4,3,2,1,0:T(8,128)(2,1)S(1)}, u32[]{:S(2)}, u32[]{:S(2)}) %collective-permute-start.13) | collective-permute-done | bytes 294560 | tf_op jit(solution)/shard_map/ppermute | solution.py:25
  324.3 4.8 collective-permute-start.14
  329.1 41.0 %all-reduce.3 = (f32[768]{0:T(1024)S(1)}, f32[768]{0:T(1024)}, f32[80,2]{0,1:T(2,128)S(1)}) all-reduce(f32[768]{0:T(1024)S(1)} %select_add_fusion.5, f32[768]{0:T(1024)S(1)} %select_add_fusion.4, f32[80,2]{0,1:T(2,128)} %fusion.124), channel_id=2, replica_groups=mesh['section'=2,'dp'=16] {'dp'}, use_global_device_ids=true, to_apply=%region_32.33.clone | all-reduce | flops 1696 | bytes 13568
  373.1 2.1 maximum_bitcast_fusion.1
  377.7 5.0 %collective-permute-start.16 = (bf16[1,1,1,48,767]{4,3,2,1,0:T(8,128)(2,1)S(1)}, bf16[1,1,1,48,767]{4,3,2,1,0:T(8,128)(2,1)S(1)}, u32[]{:S(2)}, u32[]{:S(2)}) collective-permute-start(bf16[1,1,1,48,767]{4,3,2,1,0:T(8,128)(2,1)S(1)} %get-tuple-element.44), channel_id=1, source_target_pairs={{0,4},{1,5},{2,6},{3,7},{4,8},{5,9},{6,10},{7,11},{8,12},{9,13},{1... | collective-permute-start | bytes 220904 | tf_op jit(solution)/shard_map/ppermute | solution.py:49
  386.3 4.3 collective-permute-done.19
  392.2 3.0 convert_add_fusion.2
  395.4 4.4 convert_add_fusion
  400.0 4.0 collective-permute-start.29
  404.7 2.6 convert_add_fusion.1
  409.8 2.8 collective-permute-start.6
  412.6 5.1 %collective-permute-done.29 = bf16[1,2,1,192,767]{4,3,2,1,0:T(8,128)(2,1)S(1)} collective-permute-done((bf16[1,2,1,192,767]{4,3,2,1,0:T(8,128)(2,1)S(1)}, bf16[1,2,1,192,767]{4,3,2,1,0:T(8,128)(2,1)S(1)}, u32[]{:S(2)}, u32[]{:S(2)}) %collective-permute-start.29) | collective-permute-done | bytes 589088 | tf_op jit(solution)/shard_map/ppermute | solution.py:49
  418.5 11.8 %collective-permute-done.21 = bf16[1,1,2,48,3072]{4,3,2,1,0:T(8,128)(2,1)S(1)} collective-permute-done((bf16[1,1,2,48,3072]{4,3,2,1,0:T(8,128)(2,1)S(1)}, bf16[1,1,2,48,3072]{4,3,2,1,0:T(8,128)(2,1)S(1)}, u32[]{:S(2)}, u32[]{:S(2)}) %collective-permute-start.21) | collective-permute-done | bytes 589856 | tf_op jit(solution)/shard_map/ppermute | solution.py:49
  430.3 4.4 collective-permute-start.30
  435.1 4.4 collective-permute-start.22
  441.5 3.9 collective-permute-done.30
  446.3 8.7 %collective-permute-done.22 = bf16[1,1,2,48,3072]{4,3,2,1,0:T(8,128)(2,1)S(1)} collective-permute-done((bf16[1,1,2,48,3072]{4,3,2,1,0:T(8,128)(2,1)S(1)}, bf16[1,1,2,48,3072]{4,3,2,1,0:T(8,128)(2,1)S(1)}, u32[]{:S(2)}, u32[]{:S(2)}) %collective-permute-start.22) | collective-permute-done | bytes 589856 | tf_op jit(solution)/shard_map/ppermute | solution.py:49
  456.1 3.7 collective-permute-done.7
  460.6 5.0 %collective-permute-start.8 = (bf16[1,1,1,48,2304]{4,3,2,1,0:T(8,128)(2,1)S(1)}, bf16[1,1,1,48,2304]{4,3,2,1,0:T(8,128)(2,1)S(1)}, u32[]{:S(2)}, u32[]{:S(2)}) collective-permute-start(bf16[1,1,1,48,2304]{4,3,2,1,0:T(8,128)(2,1)S(1)} %get-tuple-element.40), channel_id=1, source_target_pairs={{0,4},{1,5},{2,6},{3,7},{4,8},{5,9},{6,10},{7,11},{8,12},{9,13},{1... | collective-permute-start | bytes 663560 | tf_op jit(solution)/shard_map/ppermute | solution.py:49
  465.6 4.6 collective-permute-start.31
  475.1 2.6 collective-permute-done.31
  479.0 6.7 %collective-permute-done.34 = bf16[1,2,1,192,767]{4,3,2,1,0:T(8,128)(2,1)S(1)} collective-permute-done((bf16[1,2,1,192,767]{4,3,2,1,0:T(8,128)(2,1)S(1)}, bf16[1,2,1,192,767]{4,3,2,1,0:T(8,128)(2,1)S(1)}, u32[]{:S(2)}, u32[]{:S(2)}) %collective-permute-start.34) | collective-permute-done | bytes 589088 | tf_op jit(solution)/shard_map/ppermute | solution.py:49
  487.3 4.8 collective-permute-done.26
  492.4 2.0 collective-permute-done.11
  496.1 2.9 collective-permute-done.27
  (530 shorter events, 146.5 us)
Async XLA Ops:
  25.7 6.8 %slice-start.13 = ((s8[4718592]{0:T(1024)(128)(4,1)}), s8[4194304]{0:T(1024)(128)(4,1)S(1)}, s32[]{:S(2)}) async-start(s8[4718592]{0:T(1024)(128)(4,1)} %bitcast.355), calls=%async_computation.13 | async-start | bytes 8388608
  35.3 13.2 %collective-permute-start = (bf16[256,767]{1,0:T(8,128)(2,1)}, bf16[256,767]{1,0:T(8,128)(2,1)}, u32[]{:S(2)}, u32[]{:S(2)}) collective-permute-start(bf16[256,767]{1,0:T(8,128)(2,1)} %fusion.108), channel_id=1, source_target_pairs={{0,16},{1,17},{2,18},{3,19},{4,20},{5,21},{6,22},{7,23},{8,24},{9,... | collective-permute-start | bytes 1178120 | tf_op jit(solution)/shard_map/ppermute | solution.py:18
  72.1 7.9 %copy-start.104 = (pred[2,256,80]{1,2,0:T(8,128)(4,1)S(1)}, pred[2,256,80]{1,2,0:T(8,128)(4,1)}, u32[]{:S(2)}) copy-start(pred[2,256,80]{1,2,0:T(8,128)(4,1)} %compare_and_fusion) | copy-start | bytes 122884
  72.1 7.9 %copy-start.128 = (f32[256]{0:T(256)S(1)}, f32[256]{0:T(256)}, u32[]{:S(2)}) copy-start(f32[256]{0:T(256)} %get-tuple-element.55) | copy-start | bytes 3076
  72.1 7.9 %copy-start.133 = (f32[80,2]{0,1:T(2,128)S(1)}, f32[80,2]{0,1:T(2,128)}, u32[]{:S(2)}) copy-start(f32[80,2]{0,1:T(2,128)} %convolution_select_fusion.1) | copy-start | bytes 1924
  72.1 8.6 %copy-start.97 = (f32[12,256]{1,0:T(8,128)S(1)}, f32[12,256]{1,0:T(8,128)}, u32[]{:S(2)}) copy-start(f32[12,256]{1,0:T(8,128)} %copy-done.96) | copy-start | bytes 36868
  72.1 8.6 %copy-start.99 = (f32[12,256]{1,0:T(8,128)S(1)}, f32[12,256]{1,0:T(8,128)}, u32[]{:S(2)}) copy-start(f32[12,256]{1,0:T(8,128)} %copy-done.98) | copy-start | bytes 36868
  72.1 9.2 %copy-start.66 = (bf16[512,767]{1,0:T(8,128)(2,1)S(1)}, bf16[512,767]{1,0:T(8,128)(2,1)}, u32[]{:S(2)}) copy-start(bf16[512,767]{1,0:T(8,128)(2,1)} %param.10) | copy-start | bytes 2356228
  78.4 2.9 collective-permute-start.1
  104.0 16.2 %copy-start.108 = (f32[256]{0:T(256)}, f32[256]{0:T(256)S(1)}, u32[]{:S(2)}) copy-start(f32[256]{0:T(256)S(1)} %get-tuple-element.54) | copy-start | bytes 3076
  104.0 10.5 %slice-start.15 = ((s8[4718592]{0:T(1024)(128)(4,1)}), s8[4194304]{0:T(1024)(128)(4,1)S(1)}, s32[]{:S(2)}) async-start(s8[4718592]{0:T(1024)(128)(4,1)} %bitcast.357), calls=%async_computation.15 | async-start | bytes 8388608
  108.3 9.7 %slice-start.21 = ((s8[4718592]{0:T(1024)(128)(4,1)}), s8[4194304]{0:T(1024)(128)(4,1)S(1)}, s32[]{:S(2)}) async-start(s8[4718592]{0:T(1024)(128)(4,1)} %bitcast.363), calls=%async_computation.21 | async-start | bytes 8388608
  149.3 8.6 %slice-start.17 = ((s8[4718592]{0:T(1024)(128)(4,1)}), s8[4194304]{0:T(1024)(128)(4,1)S(1)}, s32[]{:S(2)}) async-start(s8[4718592]{0:T(1024)(128)(4,1)} %bitcast.359), calls=%async_computation.17 | async-start | bytes 8388608
  149.6 8.4 %copy-start.87 = (bf16[256,767]{1,0:T(8,128)(2,1)}, bf16[256,767]{1,0:T(8,128)(2,1)S(1)}, u32[]{:S(2)}) copy-start(bf16[256,767]{1,0:T(8,128)(2,1)S(1)} %fusion.132) | copy-start | bytes 1178116
  149.6 8.3 %collective-permute-start.2 = (bf16[256,767]{1,0:T(8,128)(2,1)S(1)}, bf16[256,767]{1,0:T(8,128)(2,1)S(1)}, u32[]{:S(2)}, u32[]{:S(2)}) collective-permute-start(bf16[256,767]{1,0:T(8,128)(2,1)S(1)} %fusion.132), channel_id=1, source_target_pairs={{16,0},{17,1},{18,2},{19,3},{20,4},{21,5},{22,6},{23,7},{24,8},{25... | collective-permute-start | bytes 1178120 | tf_op jit(solution)/shard_map/ppermute | solution.py:18
  153.1 8.0 %slice-start.23 = ((s8[4718592]{0:T(1024)(128)(4,1)}), s8[4194304]{0:T(1024)(128)(4,1)S(1)}, s32[]{:S(2)}) async-start(s8[4718592]{0:T(1024)(128)(4,1)} %bitcast.365), calls=%async_computation.23 | async-start | bytes 8388608
  193.3 6.3 %collective-permute-start.3 = (bf16[256,767]{1,0:T(8,128)(2,1)S(1)}, bf16[256,767]{1,0:T(8,128)(2,1)S(1)}, u32[]{:S(2)}, u32[]{:S(2)}) collective-permute-start(bf16[256,767]{1,0:T(8,128)(2,1)S(1)} %get-tuple-element.25), channel_id=1, source_target_pairs={{16,0},{17,1},{18,2},{19,3},{20,4},{21,5},{22,6},{23,7},{24,8},{25... | collective-permute-start | bytes 1178120 | tf_op jit(solution)/shard_map/ppermute | solution.py:18
  195.3 7.5 %slice-start.25 = ((s8[4718592]{0:T(1024)(128)(4,1)}), s8[4194304]{0:T(1024)(128)(4,1)S(1)}, s32[]{:S(2)}) async-start(s8[4718592]{0:T(1024)(128)(4,1)} %bitcast.367), calls=%async_computation.25 | async-start | bytes 8388608
  224.1 7.9 %copy-start.34 = (f32[256,767]{1,0:T(8,128)S(1)}, f32[256,767]{1,0:T(8,128)}, u32[]{:S(2)}) copy-start(f32[256,767]{1,0:T(8,128)} %get-tuple-element.66) | copy-start | bytes 2356228
  224.2 7.9 %copy-start.69 = (f32[256,1]{1,0:T(8,128)S(1)}, f32[256,1]{1,0:T(8,128)}, u32[]{:S(2)}) copy-start(f32[256,1]{1,0:T(8,128)} %copy.97) | copy-start | bytes 3076
  224.2 168.0 %collective-permute-start.4 = (bf16[4,2,1,48,2304]{4,3,2,1,0:T(8,128)(2,1)}, bf16[4,2,1,48,2304]{4,3,2,1,0:T(8,128)(2,1)}, u32[]{:S(2)}, u32[]{:S(2)}) collective-permute-start(bf16[4,2,1,48,2304]{4,3,2,1,0:T(8,128)(2,1)} %dynamic-slice_convert_fusion.2), channel_id=1, source_target_pairs={{0,1},{1,0},{2,3},{3,2},{4,5},{5,4},{6,7},{7,6},{8,9},{9,8},{10,11... | collective-permute-start | bytes 5308424 | tf_op jit(solution)/shard_map/ppermute | solution.py:25
  228.8 18.6 %slice-start = ((s8[9437184]{0:T(1024)(128)(4,1)}), s8[4194304]{0:T(1024)(128)(4,1)S(1)}, s32[]{:S(2)}) async-start(s8[9437184]{0:T(1024)(128)(4,1)} %bitcast.289), calls=%async_computation | async-start | bytes 8388608
  228.8 18.6 %slice-start.3 = ((s8[9437184]{0:T(1024)(128)(4,1)}), s8[4194304]{0:T(1024)(128)(4,1)S(1)}, s32[]{:S(2)}) async-start(s8[9437184]{0:T(1024)(128)(4,1)} %bitcast.291), calls=%async_computation.3 | async-start | bytes 8388608
  229.6 17.7 %slice-start.1 = ((s8[9437184]{0:T(1024)(128)(4,1)}), s8[4194304]{0:T(1024)(128)(4,1)S(1)}, s32[]{:S(2)}) async-start(s8[9437184]{0:T(1024)(128)(4,1)} %bitcast.289), calls=%async_computation.1 | async-start | bytes 8388608
  229.6 17.7 %slice-start.2 = ((s8[9437184]{0:T(1024)(128)(4,1)}), s8[1048576]{0:T(1024)(128)(4,1)S(1)}, s32[]{:S(2)}) async-start(s8[9437184]{0:T(1024)(128)(4,1)} %bitcast.289), calls=%async_computation.2 | async-start | bytes 2097152
  229.6 17.7 %slice-start.4 = ((s8[9437184]{0:T(1024)(128)(4,1)}), s8[4194304]{0:T(1024)(128)(4,1)S(1)}, s32[]{:S(2)}) async-start(s8[9437184]{0:T(1024)(128)(4,1)} %bitcast.291), calls=%async_computation.4 | async-start | bytes 8388608
  229.6 17.8 %slice-start.5 = ((s8[9437184]{0:T(1024)(128)(4,1)}), s8[1048576]{0:T(1024)(128)(4,1)S(1)}, s32[]{:S(2)}) async-start(s8[9437184]{0:T(1024)(128)(4,1)} %bitcast.291), calls=%async_computation.5 | async-start | bytes 2097152
  229.6 32.0 %collective-permute-start.12 = (bf16[4,1,2,48,767]{4,3,2,1,0:T(8,128)(2,1)}, bf16[4,1,2,48,767]{4,3,2,1,0:T(8,128)(2,1)}, u32[]{:S(2)}, u32[]{:S(2)}) collective-permute-start(bf16[4,1,2,48,767]{4,3,2,1,0:T(8,128)(2,1)} %dynamic-slice_convert_fusion.8), channel_id=1, source_target_pairs={{0,2},{1,3},{2,0},{3,1},{4,6},{5,7},{6,4},{7,5},{8,10},{9,11},{10,... | collective-permute-start | bytes 1767176 | tf_op jit(solution)/shard_map/ppermute | solution.py:25
  246.4 158.3 %collective-permute-start.20 = (bf16[4,1,2,48,3072]{4,3,2,1,0:T(8,128)(2,1)}, bf16[4,1,2,48,3072]{4,3,2,1,0:T(8,128)(2,1)}, u32[]{:S(2)}, u32[]{:S(2)}) collective-permute-start(bf16[4,1,2,48,3072]{4,3,2,1,0:T(8,128)(2,1)} %dynamic-slice_convert_fusion.1), channel_id=1, source_target_pairs={{0,2},{1,3},{2,0},{3,1},{4,6},{5,7},{6,4},{7,5},{8,10},{9,11},{10,... | collective-permute-start | bytes 7077896 | tf_op jit(solution)/shard_map/ppermute | solution.py:25
  260.1 135.4 %collective-permute-start.28 = (bf16[4,2,1,192,767]{4,3,2,1,0:T(8,128)(2,1)}, bf16[4,2,1,192,767]{4,3,2,1,0:T(8,128)(2,1)}, u32[]{:S(2)}, u32[]{:S(2)}) collective-permute-start(bf16[4,2,1,192,767]{4,3,2,1,0:T(8,128)(2,1)} %dynamic-slice_convert_fusion), channel_id=1, source_target_pairs={{0,1},{1,0},{2,3},{3,2},{4,5},{5,4},{6,7},{7,6},{8,9},{9,8},{10,11... | collective-permute-start | bytes 7068680 | tf_op jit(solution)/shard_map/ppermute | solution.py:25
  262.9 66.2 %copy-start.120 = (f32[768]{0:T(1024)S(1)}, f32[768]{0:T(1024)}, u32[]{:S(2)}) copy-start(f32[768]{0:T(1024)} %get-tuple-element.9) | copy-start | bytes 9220
  262.9 66.2 %copy-start.121 = (f32[768]{0:T(1024)S(1)}, f32[768]{0:T(1024)}, u32[]{:S(2)}) copy-start(f32[768]{0:T(1024)} %get-tuple-element.11) | copy-start | bytes 9220
  262.9 66.2 %copy-start.123 = (f32[768]{0:T(1024)S(1)}, f32[768]{0:T(1024)}, u32[]{:S(2)}) copy-start(f32[768]{0:T(1024)} %get-tuple-element.13) | copy-start | bytes 9220
  263.0 59.8 %collective-permute-start.13 = (bf16[4,1,1,48,767]{4,3,2,1,0:T(8,128)(2,1)S(1)}, bf16[4,1,1,48,767]{4,3,2,1,0:T(8,128)(2,1)S(1)}, u32[]{:S(2)}, u32[]{:S(2)}) collective-permute-start(bf16[4,1,1,48,767]{4,3,2,1,0:T(8,128)(2,1)S(1)} %dynamic-slice_convert_fusion.11), channel_id=1, source_target_pairs={{0,1},{1,0},{2,3},{3,2},{4,5},{5,4},{6,7},{7,6},{8,9},{9,8},{10,11... | collective-permute-start | bytes 883592 | tf_op jit(solution)/shard_map/ppermute | solution.py:25
  324.3 46.5 %collective-permute-start.14 = (bf16[1,1,1,48,767]{4,3,2,1,0:T(8,128)(2,1)}, bf16[1,1,1,48,767]{4,3,2,1,0:T(8,128)(2,1)}, u32[]{:S(2)}, u32[]{:S(2)}) collective-permute-start(bf16[1,1,1,48,767]{4,3,2,1,0:T(8,128)(2,1)} %get-tuple-element.46), channel_id=1, source_target_pairs={{0,4},{1,5},{2,6},{3,7},{16,20},{17,21},{18,22},{19,23}} | collective-permute-start | bytes 220904 | tf_op jit(solution)/shard_map/ppermute | solution.py:49
  370.1 5.0 %collective-permute-start.17 = (bf16[1,1,1,48,767]{4,3,2,1,0:T(8,128)(2,1)}, bf16[1,1,1,48,767]{4,3,2,1,0:T(8,128)(2,1)S(1)}, u32[]{:S(2)}, u32[]{:S(2)}) collective-permute-start(bf16[1,1,1,48,767]{4,3,2,1,0:T(8,128)(2,1)} %get-tuple-element.47), channel_id=1, source_target_pairs={{12,8},{13,9},{14,10},{15,11},{28,24},{29,25},{30,26},{31,27}} | collective-permute-start | bytes 220904 | tf_op jit(solution)/shard_map/ppermute | solution.py:49
  371.8 3.7 collective-permute-start.15
  376.4 6.3 %collective-permute-start.18 = (bf16[1,1,1,48,767]{4,3,2,1,0:T(8,128)(2,1)S(1)}, bf16[1,1,1,48,767]{4,3,2,1,0:T(8,128)(2,1)S(1)}, u32[]{:S(2)}, u32[]{:S(2)}) collective-permute-start(bf16[1,1,1,48,767]{4,3,2,1,0:T(8,128)(2,1)S(1)} %get-tuple-element.45), channel_id=1, source_target_pairs={{8,4},{9,5},{10,6},{11,7},{12,8},{13,9},{14,10},{15,11},{24,20},{2... | collective-permute-start | bytes 220904 | tf_op jit(solution)/shard_map/ppermute | solution.py:49
  377.7 8.5 %collective-permute-start.16 = (bf16[1,1,1,48,767]{4,3,2,1,0:T(8,128)(2,1)S(1)}, bf16[1,1,1,48,767]{4,3,2,1,0:T(8,128)(2,1)S(1)}, u32[]{:S(2)}, u32[]{:S(2)}) collective-permute-start(bf16[1,1,1,48,767]{4,3,2,1,0:T(8,128)(2,1)S(1)} %get-tuple-element.44), channel_id=1, source_target_pairs={{0,4},{1,5},{2,6},{3,7},{4,8},{5,9},{6,10},{7,11},{8,12},{9,13},{1... | collective-permute-start | bytes 220904 | tf_op jit(solution)/shard_map/ppermute | solution.py:49
  383.7 6.9 %collective-permute-start.19 = (bf16[1,1,1,48,767]{4,3,2,1,0:T(8,128)(2,1)S(1)}, bf16[1,1,1,48,767]{4,3,2,1,0:T(8,128)(2,1)S(1)}, u32[]{:S(2)}, u32[]{:S(2)}) collective-permute-start(bf16[1,1,1,48,767]{4,3,2,1,0:T(8,128)(2,1)S(1)} %add_convert_fusion.12), channel_id=1, source_target_pairs={{4,0},{5,1},{6,2},{7,3},{8,4},{9,5},{10,6},{11,7},{12,8},{13,9},{1... | collective-permute-start | bytes 220904 | tf_op jit(solution)/shard_map/ppermute | solution.py:49
  392.2 12.5 %slice-start.10 = ((s8[9437184]{0:T(1024)(128)(4,1)}), s8[4194304]{0:T(1024)(128)(4,1)S(1)}, s32[]{:S(2)}) async-start(s8[9437184]{0:T(1024)(128)(4,1)} %bitcast.300), calls=%async_computation.10 | async-start | bytes 8388608
  392.2 12.5 %slice-start.11 = ((s8[9437184]{0:T(1024)(128)(4,1)}), s8[4194304]{0:T(1024)(128)(4,1)S(1)}, s32[]{:S(2)}) async-start(s8[9437184]{0:T(1024)(128)(4,1)} %bitcast.300), calls=%async_computation.11 | async-start | bytes 8388608
  395.3 9.4 %slice-start.12 = ((s8[9437184]{0:T(1024)(128)(4,1)}), s8[1048576]{0:T(1024)(128)(4,1)S(1)}, s32[]{:S(2)}) async-start(s8[9437184]{0:T(1024)(128)(4,1)} %bitcast.300), calls=%async_computation.12 | async-start | bytes 2097152
  395.3 14.2 %collective-permute-start.5 = (bf16[4,1,1,48,2304]{4,3,2,1,0:T(8,128)(2,1)S(1)}, bf16[4,1,1,48,2304]{4,3,2,1,0:T(8,128)(2,1)S(1)}, u32[]{:S(2)}, u32[]{:S(2)}) collective-permute-start(bf16[4,1,1,48,2304]{4,3,2,1,0:T(8,128)(2,1)S(1)} %dynamic-slice_convert_fusion.3), channel_id=1, source_target_pairs={{0,2},{1,3},{2,0},{3,1},{4,6},{5,7},{6,4},{7,5},{8,10},{9,11},{10,... | collective-permute-start | bytes 2654216 | tf_op jit(solution)/shard_map/ppermute | solution.py:25
  400.0 17.7 %collective-permute-start.29 = (bf16[1,2,1,192,767]{4,3,2,1,0:T(8,128)(2,1)S(1)}, bf16[1,2,1,192,767]{4,3,2,1,0:T(8,128)(2,1)S(1)}, u32[]{:S(2)}, u32[]{:S(2)}) collective-permute-start(bf16[1,2,1,192,767]{4,3,2,1,0:T(8,128)(2,1)S(1)} %get-tuple-element.34), channel_id=1, source_target_pairs={{0,4},{1,5},{2,6},{3,7},{16,20},{17,21},{18,22},{19,23}} | collective-permute-start | bytes 1767176 | tf_op jit(solution)/shard_map/ppermute | solution.py:49
  404.0 35.6 %collective-permute-start.32 = (bf16[1,2,1,192,767]{4,3,2,1,0:T(8,128)(2,1)S(1)}, bf16[1,2,1,192,767]{4,3,2,1,0:T(8,128)(2,1)S(1)}, u32[]{:S(2)}, u32[]{:S(2)}) collective-permute-start(bf16[1,2,1,192,767]{4,3,2,1,0:T(8,128)(2,1)S(1)} %get-tuple-element.35), channel_id=1, source_target_pairs={{12,8},{13,9},{14,10},{15,11},{28,24},{29,25},{30,26},{31,27}} | collective-permute-start | bytes 1767176 | tf_op jit(solution)/shard_map/ppermute | solution.py:49
  407.5 22.8 %collective-permute-start.21 = (bf16[1,1,2,48,3072]{4,3,2,1,0:T(8,128)(2,1)S(1)}, bf16[1,1,2,48,3072]{4,3,2,1,0:T(8,128)(2,1)S(1)}, u32[]{:S(2)}, u32[]{:S(2)}) collective-permute-start(bf16[1,1,2,48,3072]{4,3,2,1,0:T(8,128)(2,1)S(1)} %get-tuple-element.38), channel_id=1, source_target_pairs={{0,4},{1,5},{2,6},{3,7},{16,20},{17,21},{18,22},{19,23}} | collective-permute-start | bytes 1769480 | tf_op jit(solution)/shard_map/ppermute | solution.py:49
  408.9 37.5 %collective-permute-start.24 = (bf16[1,1,2,48,3072]{4,3,2,1,0:T(8,128)(2,1)S(1)}, bf16[1,1,2,48,3072]{4,3,2,1,0:T(8,128)(2,1)S(1)}, u32[]{:S(2)}, u32[]{:S(2)}) collective-permute-start(bf16[1,1,2,48,3072]{4,3,2,1,0:T(8,128)(2,1)S(1)} %get-tuple-element.39), channel_id=1, source_target_pairs={{12,8},{13,9},{14,10},{15,11},{28,24},{29,25},{30,26},{31,27}} | collective-permute-start | bytes 1769480 | tf_op jit(solution)/shard_map/ppermute | solution.py:49
  409.8 25.3 %collective-permute-start.6 = (bf16[1,1,1,48,2304]{4,3,2,1,0:T(8,128)(2,1)S(1)}, bf16[1,1,1,48,2304]{4,3,2,1,0:T(8,128)(2,1)S(1)}, u32[]{:S(2)}, u32[]{:S(2)}) collective-permute-start(bf16[1,1,1,48,2304]{4,3,2,1,0:T(8,128)(2,1)S(1)} %get-tuple-element.42), channel_id=1, source_target_pairs={{0,4},{1,5},{2,6},{3,7},{16,20},{17,21},{18,22},{19,23}} | collective-permute-start | bytes 663560 | tf_op jit(solution)/shard_map/ppermute | solution.py:49
  417.7 38.4 %collective-permute-start.9 = (bf16[1,1,1,48,2304]{4,3,2,1,0:T(8,128)(2,1)S(1)}, bf16[1,1,1,48,2304]{4,3,2,1,0:T(8,128)(2,1)S(1)}, u32[]{:S(2)}, u32[]{:S(2)}) collective-permute-start(bf16[1,1,1,48,2304]{4,3,2,1,0:T(8,128)(2,1)S(1)} %get-tuple-element.43), channel_id=1, source_target_pairs={{12,8},{13,9},{14,10},{15,11},{28,24},{29,25},{30,26},{31,27}} | collective-permute-start | bytes 663560 | tf_op jit(solution)/shard_map/ppermute | solution.py:49
  430.3 15.0 %collective-permute-start.30 = (bf16[1,2,1,192,767]{4,3,2,1,0:T(8,128)(2,1)S(1)}, bf16[1,2,1,192,767]{4,3,2,1,0:T(8,128)(2,1)S(1)}, u32[]{:S(2)}, u32[]{:S(2)}) collective-permute-start(bf16[1,2,1,192,767]{4,3,2,1,0:T(8,128)(2,1)S(1)} %add_convert_fusion.3), channel_id=1, source_target_pairs={{0,4},{1,5},{2,6},{3,7},{4,8},{5,9},{6,10},{7,11},{16,20},{17,21},... | collective-permute-start | bytes 1767176 | tf_op jit(solution)/shard_map/ppermute | solution.py:49
  435.1 20.0 %collective-permute-start.22 = (bf16[1,1,2,48,3072]{4,3,2,1,0:T(8,128)(2,1)S(1)}, bf16[1,1,2,48,3072]{4,3,2,1,0:T(8,128)(2,1)S(1)}, u32[]{:S(2)}, u32[]{:S(2)}) collective-permute-start(bf16[1,1,2,48,3072]{4,3,2,1,0:T(8,128)(2,1)S(1)} %add_convert_fusion.7), channel_id=1, source_target_pairs={{0,4},{1,5},{2,6},{3,7},{4,8},{5,9},{6,10},{7,11},{16,20},{17,21},... | collective-permute-start | bytes 1769480 | tf_op jit(solution)/shard_map/ppermute | solution.py:49
  439.6 20.2 %collective-permute-start.7 = (bf16[1,1,1,48,2304]{4,3,2,1,0:T(8,128)(2,1)S(1)}, bf16[1,1,1,48,2304]{4,3,2,1,0:T(8,128)(2,1)S(1)}, u32[]{:S(2)}, u32[]{:S(2)}) collective-permute-start(bf16[1,1,1,48,2304]{4,3,2,1,0:T(8,128)(2,1)S(1)} %add_convert_fusion.11), channel_id=1, source_target_pairs={{0,4},{1,5},{2,6},{3,7},{4,8},{5,9},{6,10},{7,11},{16,20},{17,21},... | collective-permute-start | bytes 663560 | tf_op jit(solution)/shard_map/ppermute | solution.py:49
  445.6 24.6 %collective-permute-start.33 = (bf16[1,2,1,192,767]{4,3,2,1,0:T(8,128)(2,1)S(1)}, bf16[1,2,1,192,767]{4,3,2,1,0:T(8,128)(2,1)S(1)}, u32[]{:S(2)}, u32[]{:S(2)}) collective-permute-start(bf16[1,2,1,192,767]{4,3,2,1,0:T(8,128)(2,1)S(1)} %get-tuple-element.33), channel_id=1, source_target_pairs={{8,4},{9,5},{10,6},{11,7},{12,8},{13,9},{14,10},{15,11},{24,20},{2... | collective-permute-start | bytes 1767176 | tf_op jit(solution)/shard_map/ppermute | solution.py:49
  455.4 16.9 %collective-permute-start.25 = (bf16[1,1,2,48,3072]{4,3,2,1,0:T(8,128)(2,1)S(1)}, bf16[1,1,2,48,3072]{4,3,2,1,0:T(8,128)(2,1)S(1)}, u32[]{:S(2)}, u32[]{:S(2)}) collective-permute-start(bf16[1,1,2,48,3072]{4,3,2,1,0:T(8,128)(2,1)S(1)} %get-tuple-element.37), channel_id=1, source_target_pairs={{8,4},{9,5},{10,6},{11,7},{12,8},{13,9},{14,10},{15,11},{24,20},{2... | collective-permute-start | bytes 1769480 | tf_op jit(solution)/shard_map/ppermute | solution.py:49
  459.9 13.8 %collective-permute-start.10 = (bf16[1,1,1,48,2304]{4,3,2,1,0:T(8,128)(2,1)S(1)}, bf16[1,1,1,48,2304]{4,3,2,1,0:T(8,128)(2,1)S(1)}, u32[]{:S(2)}, u32[]{:S(2)}) collective-permute-start(bf16[1,1,1,48,2304]{4,3,2,1,0:T(8,128)(2,1)S(1)} %get-tuple-element.41), channel_id=1, source_target_pairs={{8,4},{9,5},{10,6},{11,7},{12,8},{13,9},{14,10},{15,11},{24,20},{2... | collective-permute-start | bytes 663560 | tf_op jit(solution)/shard_map/ppermute | solution.py:49
  460.6 31.8 %collective-permute-start.8 = (bf16[1,1,1,48,2304]{4,3,2,1,0:T(8,128)(2,1)S(1)}, bf16[1,1,1,48,2304]{4,3,2,1,0:T(8,128)(2,1)S(1)}, u32[]{:S(2)}, u32[]{:S(2)}) collective-permute-start(bf16[1,1,1,48,2304]{4,3,2,1,0:T(8,128)(2,1)S(1)} %get-tuple-element.40), channel_id=1, source_target_pairs={{0,4},{1,5},{2,6},{3,7},{4,8},{5,9},{6,10},{7,11},{8,12},{9,13},{1... | collective-permute-start | bytes 663560 | tf_op jit(solution)/shard_map/ppermute | solution.py:49
  465.6 12.1 %collective-permute-start.31 = (bf16[1,2,1,192,767]{4,3,2,1,0:T(8,128)(2,1)S(1)}, bf16[1,2,1,192,767]{4,3,2,1,0:T(8,128)(2,1)S(1)}, u32[]{:S(2)}, u32[]{:S(2)}) collective-permute-start(bf16[1,2,1,192,767]{4,3,2,1,0:T(8,128)(2,1)S(1)} %get-tuple-element.32), channel_id=1, source_target_pairs={{0,4},{1,5},{2,6},{3,7},{4,8},{5,9},{6,10},{7,11},{8,12},{9,13},{1... | collective-permute-start | bytes 1767176 | tf_op jit(solution)/shard_map/ppermute | solution.py:49
  470.2 17.1 %collective-permute-start.23 = (bf16[1,1,2,48,3072]{4,3,2,1,0:T(8,128)(2,1)S(1)}, bf16[1,1,2,48,3072]{4,3,2,1,0:T(8,128)(2,1)S(1)}, u32[]{:S(2)}, u32[]{:S(2)}) collective-permute-start(bf16[1,1,2,48,3072]{4,3,2,1,0:T(8,128)(2,1)S(1)} %get-tuple-element.36), channel_id=1, source_target_pairs={{0,4},{1,5},{2,6},{3,7},{4,8},{5,9},{6,10},{7,11},{8,12},{9,13},{1... | collective-permute-start | bytes 1769480 | tf_op jit(solution)/shard_map/ppermute | solution.py:49
  472.3 13.5 %collective-permute-start.34 = (bf16[1,2,1,192,767]{4,3,2,1,0:T(8,128)(2,1)S(1)}, bf16[1,2,1,192,767]{4,3,2,1,0:T(8,128)(2,1)S(1)}, u32[]{:S(2)}, u32[]{:S(2)}) collective-permute-start(bf16[1,2,1,192,767]{4,3,2,1,0:T(8,128)(2,1)S(1)} %add_convert_fusion), channel_id=1, source_target_pairs={{4,0},{5,1},{6,2},{7,3},{8,4},{9,5},{10,6},{11,7},{12,8},{13,9},{1... | collective-permute-start | bytes 1767176 | tf_op jit(solution)/shard_map/ppermute | solution.py:49
  473.7 18.3 %collective-permute-start.26 = (bf16[1,1,2,48,3072]{4,3,2,1,0:T(8,128)(2,1)S(1)}, bf16[1,1,2,48,3072]{4,3,2,1,0:T(8,128)(2,1)S(1)}, u32[]{:S(2)}, u32[]{:S(2)}) collective-permute-start(bf16[1,1,2,48,3072]{4,3,2,1,0:T(8,128)(2,1)S(1)} %add_convert_fusion.4), channel_id=1, source_target_pairs={{4,0},{5,1},{6,2},{7,3},{8,4},{9,5},{10,6},{11,7},{12,8},{13,9},{1... | collective-permute-start | bytes 1769480 | tf_op jit(solution)/shard_map/ppermute | solution.py:49
  477.7 16.7 %collective-permute-start.11 = (bf16[1,1,1,48,2304]{4,3,2,1,0:T(8,128)(2,1)S(1)}, bf16[1,1,1,48,2304]{4,3,2,1,0:T(8,128)(2,1)S(1)}, u32[]{:S(2)}, u32[]{:S(2)}) collective-permute-start(bf16[1,1,1,48,2304]{4,3,2,1,0:T(8,128)(2,1)S(1)} %add_convert_fusion.8), channel_id=1, source_target_pairs={{4,0},{5,1},{6,2},{7,3},{8,4},{9,5},{10,6},{11,7},{12,8},{13,9},{1... | collective-permute-start | bytes 663560 | tf_op jit(solution)/shard_map/ppermute | solution.py:49
  486.0 9.3 %collective-permute-start.35 = (bf16[1,1,1,192,767]{4,3,2,1,0:T(8,128)(2,1)S(1)}, bf16[1,1,1,192,767]{4,3,2,1,0:T(8,128)(2,1)S(1)}, u32[]{:S(2)}, u32[]{:S(2)}) collective-permute-start(bf16[1,1,1,192,767]{4,3,2,1,0:T(8,128)(2,1)S(1)} %dynamic-slice_convert_fusion.9), channel_id=1, source_target_pairs={{0,2},{1,3},{2,0},{3,1},{4,6},{5,7},{6,4},{7,5},{8,10},{9,11},{10,... | collective-permute-start | bytes 883592 | tf_op jit(solution)/shard_map/ppermute | solution.py:25
  492.3 6.8 %collective-permute-start.27 = (bf16[1,1,1,48,3072]{4,3,2,1,0:T(8,128)(2,1)S(1)}, bf16[1,1,1,48,3072]{4,3,2,1,0:T(8,128)(2,1)S(1)}, u32[]{:S(2)}, u32[]{:S(2)}) collective-permute-start(bf16[1,1,1,48,3072]{4,3,2,1,0:T(8,128)(2,1)S(1)} %dynamic-slice_convert_fusion.10), channel_id=1, source_target_pairs={{0,1},{1,0},{2,3},{3,2},{4,5},{5,4},{6,7},{7,6},{8,9},{9,8},{10,11... | collective-permute-start | bytes 884744 | tf_op jit(solution)/shard_map/ppermute | solution.py:25
  (133 other events, 439.5 us)
